TPU v7x, 32 devices: a whole 2x2x4 slice. The times are simulated.
32 devices in a mesh: fc: 8 (over z, core), tok: 4 (over y, x).
Axes of the slice: x: 2, y: 2, z: 4, core: 2. Of those that a mesh axis runs over, the one named last changes fastest.
Arguments:
- tokens: bfloat16 [8, 32, 128, 1024], P('fc', 'tok'), may hold values from -6 to 6
- slot_keys: bfloat16 [1024, 256], replicated, may hold values from -2 to 2
- norm_gain: float32 [1024], replicated, may hold values from 0.25 to 1.75
- slot_gain: float32 [1024], replicated, may hold values from 0.25 to 1.75
- w_in: bfloat16 [64, 1024, 512], P(('fc', 'tok')), may hold values from -0.1875 to 0.1875
- w_out: bfloat16 [64, 512, 1024], P(('fc', 'tok')), may hold values from -0.25 to 0.25
- conv_weight: float32 [7, 7, 1024], replicated, may hold values from -0.875 to 0.875
- ln_gain: float32 [1024], replicated, may hold values from 0.25 to 1.75
- proj: bfloat16 [1024, 1024], replicated, may hold values from -0.1875 to 0.1875
- layer_scale: float32 [1024], replicated, may hold values from 0.25 to 1.75
Outputs:
- fields: bfloat16 [8, 32, 128, 1024], P('fc', 'tok')
All inputs are finite; a program needn't handle non-finite values.
Results may differ from a plain program's by a relative error of at most 0.008.
The roundings to bfloat16 on the way count: a program that leaves them out, or rounds other values in their place, can miss the bound.
Values may be sent and summed in bfloat16 or wider, within the bound.
No kernel may reach another device: no remote copies, remote signals or barrier semaphores. Data moves between devices by JAX's collectives and lax.ppermute only.
A program may use at most 64 MiB of HBM per device.

v0:
```python
import jax
import jax.numpy as jnp
from jax import lax
from jax.sharding import PartitionSpec as P


def with_halo(block, sides, width):
    for axis, dim in sides:
        count = lax.axis_size(axis)
        forward = [(i, i + 1) for i in range(count - 1)]
        backward = [(target, source) for source, target in forward]
        low = lax.ppermute(
            lax.slice_in_dim(block, block.shape[dim] - width, None, axis=dim), axis, forward
        )
        high = lax.ppermute(lax.slice_in_dim(block, 0, width, axis=dim), axis, backward)
        block = jnp.concatenate([low, block, high], axis=dim)
    return block


def rms_scale(value, gain):
    return value * lax.rsqrt(jnp.mean(value * value, axis=-1, keepdims=True) + 1e-06) * gain


def local(
    tokens, slot_keys, norm_gain, slot_gain, w_in, w_out, conv_weight, ln_gain, proj, layer_scale
):
    rows = tokens.shape[1]
    cols = tokens.shape[2]
    width = tokens.shape[3]
    count_fc = lax.axis_size("fc")
    count_tok = lax.axis_size("tok")
    slot_total = slot_keys.shape[1]
    slot_dev = slot_total // (count_fc * count_tok)
    cells = tokens.reshape(rows * cols, width)
    normed = rms_scale(cells.astype(jnp.float32), norm_gain).astype(jnp.bfloat16)
    logits = jnp.dot(normed, slot_keys, preferred_element_type=jnp.float32)
    peak = lax.pmax(jnp.max(logits, axis=0), "tok")
    shifted = jnp.exp(logits - peak)
    dispatch = shifted.astype(jnp.bfloat16)
    numer = lax.dot_general(
        dispatch, cells, (((0,), (0,)), ((), ())), preferred_element_type=jnp.float32
    )
    numer = numer.reshape(count_fc, count_tok * slot_dev, width)
    numer = lax.psum_scatter(
        numer.astype(jnp.bfloat16), "tok", scatter_dimension=1, tiled=True
    ).astype(jnp.float32)
    local_in = rms_scale(numer, slot_gain).astype(jnp.bfloat16)
    slot_in = lax.all_to_all(local_in, "fc", split_axis=0, concat_axis=0, tiled=True)
    grouped = slot_in.reshape(count_fc, w_in.shape[0], slot_dev // w_in.shape[0], width)
    hidden = jax.nn.gelu(
        jnp.einsum("mesd,edf->mesf", grouped, w_in, preferred_element_type=jnp.float32)
    ).astype(jnp.bfloat16)
    expert_out = jnp.einsum(
        "mesf,efd->mesd", hidden, w_out, preferred_element_type=jnp.float32
    ).astype(jnp.bfloat16)
    expert_out = expert_out.reshape(count_fc, slot_dev, width)
    returned = lax.all_to_all(expert_out, "fc", split_axis=0, concat_axis=0, tiled=True)
    every_slot = lax.all_gather(returned, "tok", axis=1, tiled=True).reshape(slot_total, width)
    combine = jax.nn.softmax(logits, axis=-1).astype(jnp.bfloat16)
    mixed = jnp.dot(combine, every_slot, preferred_element_type=jnp.float32)
    state = (cells.astype(jnp.float32) + mixed).astype(jnp.bfloat16).reshape(rows, cols, width)
    padded = with_halo(state, (("tok", 0),), 3)
    padded = jnp.concatenate([padded[:, cols - 3 :], padded, padded[:, :3]], axis=1)
    conv = jnp.zeros((rows, cols, width), jnp.float32)
    for row_tap in range(7):
        for col_tap in range(7):
            conv = (
                conv
                + padded[row_tap : row_tap + rows, col_tap : col_tap + cols].astype(jnp.float32)
                * conv_weight[row_tap, col_tap]
            )
    center = conv - jnp.mean(conv, axis=-1, keepdims=True)
    spread = jnp.mean(center * center, axis=-1, keepdims=True)
    normal = (center * lax.rsqrt(spread + 1e-06) * ln_gain).astype(jnp.bfloat16)
    branch = jnp.dot(normal.reshape(rows * cols, width), proj, preferred_element_type=jnp.float32)
    result = state.reshape(rows * cols, width).astype(jnp.float32) + layer_scale * jax.nn.gelu(
        branch
    )
    return result.astype(jnp.bfloat16).reshape(1, rows, cols, width)


def solution(mesh):
    return jax.shard_map(
        local,
        mesh=mesh,
        in_specs=(
            P("fc", "tok", None, None),
            P(),
            P(),
            P(),
            P(("fc", "tok"), None, None),
            P(("fc", "tok"), None, None),
            P(),
            P(),
            P(),
            P(),
        ),
        out_specs=P("fc", "tok", None, None),
        check_vma=False,
    )
```

profile of v0, /device:TPU:4, one launch (start us, length us, event | category | flops | bytes accessed | tf_op | source)
XLA Modules:
  0.0 195.9 jit_solution(10661281492974501635)
XLA Ops:
  6.5 0.0 copy-start
  6.5 0.0 all-reduce.3.cloned.1.call-start
  6.5 2.2 %multiply_reduce_fusion.1 = f32[8,128]{1,0:T(8,128)S(1)} fusion(bf16[1,8,128,1024]{3,2,1,0:T(8,128)(2,1)} %param.10), kind=kLoop, calls=%fused_computation.19 | loop fusion | flops 3144704 | bytes 2101248 | tf_op jit(solution)/shard_map/reduce_sum | solution.py:21
  8.8 2.6 %fusion.66 = (f32[1024]{0:T(1024)S(1)}, f32[1024,256]{0,1:T(8,128)S(1)}) fusion(bf16[1024,256]{1,0:T(8,128)(2,1)} %param.11, bf16[1024,1024]{1,0:T(8,128)(2,1)} %bitcast.107, f32[1024]{0:T(1024)} %param.12, f32[1024]{0:T(1024)S(1)} %rsqrt_bitcast_fusion), kind=kOutput, calls=%fused_computation.87 | convolution fusion | flops 541326336 | bytes 3682304 | tf_op jit(solution)/shard_map/dot_general | solution.py:36
  11.4 0.0 copy-start.5
  11.4 0.0 copy-start.2
  11.4 0.3 fusion.33
  11.7 9.0 %pmax.7 = f32[256]{0:T(256)S(1)} all-reduce(f32[256]{0:T(256)S(1)} %get-tuple-element.6), channel_id=1, replica_groups=mesh['fc'=8,'tok'=4] {'tok'}, use_global_device_ids=true, to_apply=%region_4.0 | all-reduce | flops 256 | bytes 2048 | tf_op jit(solution)/shard_map/pmax | solution.py:37
  20.6 0.2 exponential_convert_fusion
  20.8 3.1 %convolution_convert_fusion = bf16[8,32,1024]{2,1,0:T(8,128)(2,1)} fusion(bf16[8,32,1024]{2,1,0:T(8,128)(2,1)S(1)} %bitcast.116, bf16[1024,1024,1]{1,0,2:T(8,128)(2,1)} %bitcast.108), kind=kOutput, calls=%fused_computation.47 | convolution fusion | flops 537133056 | bytes 3145728 | tf_op jit(solution)/shard_map/dot_general | solution.py:40
  23.9 0.0 all-reduce.3.cloned.1.call-update
  24.0 0.0 copy-done.5
  24.0 0.7 dynamic-slice
  25.3 44.3 %all-reduce.3.cloned.1.call-done = bf16[8,32,1024]{2,1,0:T(8,128)(2,1)} async-done(((bf16[8,32,1024]{2,1,0:T(8,128)(2,1)}), bf16[8,32,1024]{2,1,0:T(8,128)(2,1)}) %all-reduce.3.cloned.1.call-update) | async-done | bytes 524304
  69.6 1.0 fusion.36
  70.6 0.0 copy-done.2
  70.6 1.0 fusion.38
  71.7 11.2 %all_to_all.10 = bf16[8,8,1024]{2,1,0:T(8,128)(2,1)S(1)} all-to-all(bf16[8,8,1024]{2,1,0:T(8,128)(2,1)S(1)} %fusion.38), channel_id=1, replica_groups=mesh['fc'=8,'tok'=4] {'fc'}, dimensions={0} | all-to-all | bytes 262144 | tf_op jit(solution)/shard_map/all_to_all | solution.py:48
  82.8 0.1 copy.14
  82.9 3.0 %fusion.27 = bf16[2,8,4,1024]{3,1,2,0:T(8,128)(2,1)S(1)} fusion(bf16[2,512,1024]{2,1,0:T(8,128)(2,1)} %param.15, bf16[8,2,4,1024]{3,0,2,1:T(8,128)(2,1)S(1)} %bitcast.114, bf16[2,1024,512]{2,1,0:T(8,128)(2,1)} %param.14), kind=kOutput, calls=%fused_computation.48 | convolution fusion | flops 134578176 | bytes 4456448 | tf_op jit(solution)/shard_map/mesf,efd->mesd/dot_general | solution.py:53
  86.0 0.1 copy.15
  86.0 9.3 %all_to_all.11 = bf16[8,8,1024]{2,1,0:T(8,128)(2,1)S(1)} all-to-all(bf16[8,8,1024]{2,1,0:T(8,128)(2,1)S(1)} %copy.15), channel_id=1, replica_groups=mesh['fc'=8,'tok'=4] {'fc'}, dimensions={0} | all-to-all | bytes 262144 | tf_op jit(solution)/shard_map/all_to_all | solution.py:57
  95.3 9.2 %all_gather.3 = bf16[8,32,1024]{2,1,0:T(8,128)(2,1)S(1)} all-gather(bf16[8,8,1024]{2,1,0:T(8,128)(2,1)S(1)} %all_to_all.11), channel_id=1, replica_groups=mesh['fc'=8,'tok'=4] {'tok'}, dimensions={1}, use_global_device_ids=true | all-gather | bytes 655360 | tf_op jit(solution)/shard_map/all_gather | solution.py:58
  104.5 0.0 copy-start.1
  104.5 2.4 %fusion.2 = bf16[1024,1024]{1,0:T(8,128)(2,1)S(1)} fusion(bf16[1024,1024]{1,0:T(8,128)(2,1)} %bitcast.109, bf16[256,1024]{1,0:T(8,128)(2,1)S(1)} %bitcast.113, f32[1024,256]{0,1:T(8,128)S(1)} %get-tuple-element.63, f32[1024]{0:T(1024)S(1)} %get-tuple-element.5, f32[1024]{0:T(1024)S(1)} %get-tuple-element.62), kind=kOutput, calls=%fused_computation.5 | convolution fusion | flops 540803072 | bytes 5775360 | tf_op jit(solution)/shard_map/dot_general | solution.py:60
  106.9 0.1 fusion.62
  107.0 3.4 %collective-permute-start.1 = (bf16[3,128,1024]{2,1,0:T(8,128)(2,1)S(1)}, bf16[3,128,1024]{2,1,0:T(8,128)(2,1)S(1)}, u32[]{:S(2)}, u32[]{:S(2)}) collective-permute-start(bf16[3,128,1024]{2,1,0:T(8,128)(2,1)S(1)} %bitcast.112), channel_id=1, source_target_pairs={{1,0},{2,1},{3,2},{5,4},{6,5},{7,6},{9,8},{10,9},{11,10},{13,12},{... | collective-permute-start | bytes 2359304 | tf_op jit(solution)/shard_map/ppermute | solution.py:15
  110.4 2.7 %collective-permute-start = (bf16[3,128,1024]{2,1,0:T(8,128)(2,1)S(1)}, bf16[3,128,1024]{2,1,0:T(8,128)(2,1)S(1)}, u32[]{:S(2)}, u32[]{:S(2)}) collective-permute-start(bf16[3,128,1024]{2,1,0:T(8,128)(2,1)S(1)} %bitcast.111), channel_id=1, source_target_pairs={{0,1},{1,2},{2,3},{4,5},{5,6},{6,7},{8,9},{9,10},{10,11},{12,13},{... | collective-permute-start | bytes 2359304 | tf_op jit(solution)/shard_map/ppermute | solution.py:12
  113.1 0.0 copy-done.1
  113.2 0.1 fusion.63
  113.2 0.1 fusion.64
  113.3 15.1 %collective-permute-done.1 = bf16[3,128,1024]{2,1,0:T(8,128)(2,1)S(1)} collective-permute-done((bf16[3,128,1024]{2,1,0:T(8,128)(2,1)S(1)}, bf16[3,128,1024]{2,1,0:T(8,128)(2,1)S(1)}, u32[]{:S(2)}, u32[]{:S(2)}) %collective-permute-start.1) | collective-permute-done | bytes 786464 | tf_op jit(solution)/shard_map/ppermute | solution.py:15
  128.4 15.2 %collective-permute-done = bf16[3,128,1024]{2,1,0:T(8,128)(2,1)S(1)} collective-permute-done((bf16[3,128,1024]{2,1,0:T(8,128)(2,1)S(1)}, bf16[3,128,1024]{2,1,0:T(8,128)(2,1)S(1)}, u32[]{:S(2)}, u32[]{:S(2)}) %collective-permute-start) | collective-permute-done | bytes 786464 | tf_op jit(solution)/shard_map/ppermute | solution.py:12
  143.6 2.3 %fusion.14 = (bf16[14,131,1024]{2,1,0:T(8,128)(2,1)S(1)}, bf16[14,131,1024]{2,1,0:T(8,128)(2,1)S(1)}) fusion(bf16[3,128,1024]{2,1,0:T(8,128)(2,1)S(1)} %collective-permute-done.1, bf16[8,128,1024]{2,1,0:T(8,128)(2,1)S(1)} %bitcast.105, bf16[3,128,1024]{2,1,0:T(8,128)(2,1)S(1)} %collective-permute-done), kind=kLoop, calls=%fused_computation.24 | loop fusion | flops 45072384 | bytes 11182080 | tf_op jit(solution)/shard_map/concatenate | solution.py:63
  145.9 37.1 %fusion.61 = (f32[8,128]{1,0:T(8,128)S(1)}, f32[8,128,1024]{2,1,0:T(8,128)S(1)}) fusion(f32[1024]{0:T(1024)S(1)} %bitcast.126, bf16[14,131,1024]{2,1,0:T(8,128)(2,1)S(1)} %get-tuple-element.10, f32[1024]{0:T(1024)S(1)} %bitcast.127, f32[1024]{0:T(1024)S(1)} %bitcast.129, f32[1024]{0:T(1024)S(1)} %bitcast.130, ...), kind=kLoop, calls=%fused_computation.82 | loop fusion | flops 160431104 | bytes 96149504 | tf_op jit(solution)/shard_map/reduce_sum | solution.py:72
  183.0 0.0 copy-start.3
  183.0 0.5 multiply_reduce_fusion
  183.6 0.0 copy-start.4
  183.6 0.1 copy-done.3
  183.7 0.6 multiply_convert_fusion
  184.3 0.0 copy-done
  184.3 0.0 copy-done.4
  184.3 4.8 %fusion.12 = bf16[1024,1024]{1,0:T(8,128)(2,1)} fusion(bf16[1024,1024]{1,0:T(8,128)(2,1)S(1)} %fusion.2, f32[1024]{0:T(1024)S(1)} %copy-done.4, bf16[1024,1024]{1,0:T(8,128)(2,1)S(1)} %bitcast.110, bf16[1024,1024]{1,0:T(8,128)(2,1)S(1)} %copy-done), kind=kOutput, calls=%fused_computation.15 | convolution fusion | flops 2160066560 | bytes 8392704 | tf_op jit(solution)/shard_map/dot_general | solution.py:75
  (5 shorter events, 0.1 us)
Async XLA Ops:
  6.5 177.7 %copy-start = (bf16[1024,1024]{1,0:T(8,128)(2,1)S(1)}, bf16[1024,1024]{1,0:T(8,128)(2,1)}, u32[]{:S(2)}) copy-start(bf16[1024,1024]{1,0:T(8,128)(2,1)} %param.18) | copy-start | bytes 6291460
  6.5 63.1 %all-reduce.3.cloned.1.call-start = ((), (), s32[]{:S(2)}) async-start(), calls=%async_computation.2 | async-start | bytes 1048576
  11.4 12.6 %copy-start.5 = (u32[32]{0:T(128)S(1)}, u32[32]{0:T(128)}, u32[]{:S(2)}) copy-start(u32[32]{0:T(128)} %constant.34) | copy-start | bytes 388
  11.4 59.2 %copy-start.2 = (f32[1024]{0:T(1024)S(1)}, f32[1024]{0:T(1024)}, u32[]{:S(2)}) copy-start(f32[1024]{0:T(1024)} %param.13) | copy-start | bytes 12292
  104.5 8.6 %copy-start.1 = (f32[7,7,1024]{2,1,0:T(8,128)S(1)}, f32[7,7,1024]{2,1,0:T(8,128)}, u32[]{:S(2)}) copy-start(f32[7,7,1024]{2,1,0:T(8,128)} %param.16) | copy-start | bytes 602116
  107.0 21.4 %collective-permute-start.1 = (bf16[3,128,1024]{2,1,0:T(8,128)(2,1)S(1)}, bf16[3,128,1024]{2,1,0:T(8,128)(2,1)S(1)}, u32[]{:S(2)}, u32[]{:S(2)}) collective-permute-start(bf16[3,128,1024]{2,1,0:T(8,128)(2,1)S(1)} %bitcast.112), channel_id=1, source_target_pairs={{1,0},{2,1},{3,2},{5,4},{6,5},{7,6},{9,8},{10,9},{11,10},{13,12},{... | collective-permute-start | bytes 2359304 | tf_op jit(solution)/shard_map/ppermute | solution.py:15
  110.4 33.2 %collective-permute-start = (bf16[3,128,1024]{2,1,0:T(8,128)(2,1)S(1)}, bf16[3,128,1024]{2,1,0:T(8,128)(2,1)S(1)}, u32[]{:S(2)}, u32[]{:S(2)}) collective-permute-start(bf16[3,128,1024]{2,1,0:T(8,128)(2,1)S(1)} %bitcast.111), channel_id=1, source_target_pairs={{0,1},{1,2},{2,3},{4,5},{5,6},{6,7},{8,9},{9,10},{10,11},{12,13},{... | collective-permute-start | bytes 2359304 | tf_op jit(solution)/shard_map/ppermute | solution.py:12
  183.0 0.7 copy-start.3
  183.6 0.7 copy-start.4
Sparse Core Ops, SparseCore 0:
  24.1 45.4 all-reduce.2
where the time goes:
time: 196 us
  waiting for transfers between devices  74.6 us (38%)
  other arithmetic  45.2 us (23%)
  blocking collectives  38.6 us (20%)
  matrix products  15.9 us (8%)
  between operations  14.3 us (7%)
  starting transfers between devices  6.07 us (3%)
    unnamed x2, waiting for transfers between devices  44.3 us
    reduce_sum x1, other arithmetic, local(): center = conv - jnp.mean(conv, axis=-1, keepdims=True)  37.1 us
    ppermute x1, waiting for transfers between devices, with_halo(): lax.ppermute(lax.slice_in_dim(block, block.shape[dim] - width, None, axis...  15.2 us
    ppermute x1, waiting for transfers between devices, with_halo(): lax.ppermute(lax.slice_in_dim(block, 0, width, axis=dim), axis, backward)  15.1 us
    all_to_all x1, blocking collectives, local(): lax.all_to_all(local_in, 'fc', split_axis=0, concat_axis=0, tiled=True)  11.2 us
    all_to_all x1, blocking collectives, local(): lax.all_to_all(expert_out, 'fc', split_axis=0, concat_axis=0, tiled=True)  9.27 us
    all_gather x1, blocking collectives, local(): lax.all_gather(returned, 'tok', axis=1, tiled=True)  9.19 us
    pmax x1, blocking collectives, local(): peak = lax.pmax(jnp.max(logits, axis=0), 'tok')  8.95 us
  transfers between devices with their start and end apart: 3, of which 3 were waited for; matrix products, arithmetic and copies ran while one was open for 0% of the time, Pallas kernels for 0%

commit v1 on v0

--- a/solution.py
+++ b/solution.py
@@ -2,6 +2,18 @@
 import jax.numpy as jnp
 from jax import lax
 from jax.sharding import PartitionSpec as P
+
+
+def in_blocks(x, dim, size):
+    dims = x.shape
+    parts = x.reshape(*dims[:dim], size, dims[dim] // size, *dims[dim + 1 :])
+    return jnp.moveaxis(parts, dim, 0)
+
+
+def in_order(tiles, dim):
+    tiles = jnp.moveaxis(tiles, 0, dim)
+    lengths = tiles.shape
+    return tiles.reshape(*lengths[:dim], lengths[dim] * lengths[dim + 1], *lengths[dim + 2 :])
 
 
 def with_halo(block, sides, width):
@@ -45,7 +57,14 @@
         numer.astype(jnp.bfloat16), "tok", scatter_dimension=1, tiled=True
     ).astype(jnp.float32)
     local_in = rms_scale(numer, slot_gain).astype(jnp.bfloat16)
-    slot_in = lax.all_to_all(local_in, "fc", split_axis=0, concat_axis=0, tiled=True)
+    devices, mine = (lax.axis_size("fc"), lax.axis_index("fc"))
+    tiles = in_blocks(local_in, 0, devices)
+    outs = [tiles[mine]]
+    for step in range(1, devices):
+        sent = tiles[mine ^ step]
+        outs.append(lax.ppermute(sent, "fc", [(i_2, i_2 ^ step) for i_2 in range(devices)]))
+    tiles = jnp.stack(outs)[mine ^ jnp.arange(devices)]
+    slot_in = in_order(tiles, 0)
     grouped = slot_in.reshape(count_fc, w_in.shape[0], slot_dev // w_in.shape[0], width)
     hidden = jax.nn.gelu(
         jnp.einsum("mesd,edf->mesf", grouped, w_in, preferred_element_type=jnp.float32)

time: 196 us -> 201 us (1.026)
  blocking collectives: 38.6 us -> 29.3 us
  starting transfers between devices: 6.07 us -> 14.1 us
  waiting for transfers between devices: 74.6 us -> 80 us
    all_to_all x1 -> x0, blocking collectives: 11.2 us -> none  [local(): lax.all_to_all(local_in, 'fc', split_axis=0, concat_axis=0, tiled=True)]
    ppermute x0 -> x7, starting transfers between devices: none -> 8.06 us  [local(): lax.ppermute(sent, 'fc', [(i_2, i_2 ^ step) for i_2 in range(devices)])]
    ppermute x0 -> x7, waiting for transfers between devices: none -> 5.21 us  [local(): lax.ppermute(sent, 'fc', [(i_2, i_2 ^ step) for i_2 in range(devices)])]
  transfers between devices with their start and end apart: 3 -> 10, of which waited for: 3 -> 5; matrix products, arithmetic and copies ran while one was open for 0% -> 0% of each run, Pallas kernels for 0% -> 0%
where the time goes in v1:
time: 201 us
  waiting for transfers between devices  80 us (40%)
  other arithmetic  45.2 us (22%)
  blocking collectives  29.3 us (15%)
  matrix products  15.9 us (8%)
  between operations  14.3 us (7%)
  starting transfers between devices  14.1 us (7%)
    unnamed x2, waiting for transfers between devices  44.4 us
    reduce_sum x1, other arithmetic, local(): center = conv - jnp.mean(conv, axis=-1, keepdims=True)  37.1 us
    ppermute x1, waiting for transfers between devices, with_halo(): lax.ppermute(lax.slice_in_dim(block, block.shape[dim] - width, None, axis...  15.2 us
    ppermute x1, waiting for transfers between devices, with_halo(): lax.ppermute(lax.slice_in_dim(block, 0, width, axis=dim), axis, backward)  15.1 us
    all_to_all x1, blocking collectives, local(): lax.all_to_all(expert_out, 'fc', split_axis=0, concat_axis=0, tiled=True)  11.2 us
    all_gather x1, blocking collectives, local(): lax.all_gather(returned, 'tok', axis=1, tiled=True)  9.19 us
    pmax x1, blocking collectives, local(): peak = lax.pmax(jnp.max(logits, axis=0), 'tok')  8.95 us
    ppermute x7, starting transfers between devices, local(): lax.ppermute(sent, 'fc', [(i_2, i_2 ^ step) for i_2 in range(devices)])  8.06 us
  transfers between devices with their start and end apart: 10, of which 5 were waited for; matrix products, arithmetic and copies ran while one was open for 0% of the time, Pallas kernels for 0%

profile of v1, /device:TPU:4, one launch (start us, length us, event | category | flops | bytes accessed | tf_op | source)
XLA Modules:
  0.0 200.6 jit_solution(16844146886905436051)
XLA Ops:
  6.5 0.0 copy-start
  6.5 0.0 all-reduce.3.cloned.1.call-start
  6.5 2.2 %multiply_reduce_fusion.1 = f32[8,128]{1,0:T(8,128)S(1)} fusion(bf16[1,8,128,1024]{3,2,1,0:T(8,128)(2,1)} %param.10), kind=kLoop, calls=%fused_computation.20 | loop fusion | flops 3144704 | bytes 2101248 | tf_op jit(solution)/shard_map/reduce_sum | solution.py:33
  8.8 2.6 %fusion.67 = (f32[1024]{0:T(1024)S(1)}, f32[1024,256]{0,1:T(8,128)S(1)}) fusion(bf16[1024,256]{1,0:T(8,128)(2,1)} %param.11, bf16[1024,1024]{1,0:T(8,128)(2,1)} %bitcast.126, f32[1024]{0:T(1024)} %param.12, f32[1024]{0:T(1024)S(1)} %rsqrt_bitcast_fusion), kind=kOutput, calls=%fused_computation.106 | convolution fusion | flops 541326336 | bytes 3682304 | tf_op jit(solution)/shard_map/dot_general | solution.py:48
  11.4 0.0 copy-start.5
  11.4 0.0 copy-start.2
  11.4 0.3 fusion.33
  11.7 9.0 %pmax.7 = f32[256]{0:T(256)S(1)} all-reduce(f32[256]{0:T(256)S(1)} %get-tuple-element.6), channel_id=1, replica_groups=mesh['fc'=8,'tok'=4] {'tok'}, use_global_device_ids=true, to_apply=%region_4.0 | all-reduce | flops 256 | bytes 2048 | tf_op jit(solution)/shard_map/pmax | solution.py:49
  20.6 0.2 exponential_convert_fusion
  20.9 3.1 %convolution_convert_fusion = bf16[8,32,1024]{2,1,0:T(8,128)(2,1)} fusion(bf16[8,32,1024]{2,1,0:T(8,128)(2,1)S(1)} %bitcast.135, bf16[1024,1024,1]{1,0,2:T(8,128)(2,1)} %bitcast.127), kind=kOutput, calls=%fused_computation.48 | convolution fusion | flops 537133056 | bytes 3145728 | tf_op jit(solution)/shard_map/dot_general | solution.py:52
  23.9 0.0 all-reduce.3.cloned.1.call-update
  24.0 0.0 copy-done.5
  24.0 0.6 dynamic-slice.11
  25.2 44.4 %all-reduce.3.cloned.1.call-done = bf16[8,32,1024]{2,1,0:T(8,128)(2,1)} async-done(((bf16[8,32,1024]{2,1,0:T(8,128)(2,1)}), bf16[8,32,1024]{2,1,0:T(8,128)(2,1)}) %all-reduce.3.cloned.1.call-update) | async-done | bytes 524304
  69.6 1.0 fusion.36
  70.6 0.0 copy-done.2
  70.7 1.0 fusion.38
  71.7 0.1 collective-permute-start
  71.8 3.4 %collective-permute-start.6 = (bf16[1,8,1024]{2,1,0:T(8,128)(2,1)S(1)}, bf16[1,8,1024]{2,1,0:T(8,128)(2,1)S(1)}, u32[]{:S(2)}, u32[]{:S(2)}) collective-permute-start(bf16[1,8,1024]{2,1,0:T(8,128)(2,1)S(1)} %get-tuple-element.62), channel_id=1, source_target_pairs={{0,28},{4,24},{8,20},{12,16},{16,12},{20,8},{24,4},{28,0},{1,29},{... | collective-permute-start | bytes 49160 | tf_op jit(solution)/shard_map/ppermute | solution.py:65
  75.2 0.5 collective-permute-start.5
  75.7 0.0 collective-permute-start.4
  75.7 2.3 %collective-permute-start.3 = (bf16[1,8,1024]{2,1,0:T(8,128)(2,1)S(1)}, bf16[1,8,1024]{2,1,0:T(8,128)(2,1)S(1)}, u32[]{:S(2)}, u32[]{:S(2)}) collective-permute-start(bf16[1,8,1024]{2,1,0:T(8,128)(2,1)S(1)} %get-tuple-element.65), channel_id=1, source_target_pairs={{0,16},{4,20},{8,24},{12,28},{16,0},{20,4},{24,8},{28,12},{1,17},{... | collective-permute-start | bytes 49160 | tf_op jit(solution)/shard_map/ppermute | solution.py:65
  78.1 0.0 collective-permute-done
  78.1 1.6 collective-permute-start.1
  79.7 2.1 %collective-permute-done.1 = bf16[1,8,1024]{2,1,0:T(8,128)(2,1)S(1)} collective-permute-done((bf16[1,8,1024]{2,1,0:T(8,128)(2,1)S(1)}, bf16[1,8,1024]{2,1,0:T(8,128)(2,1)S(1)}, u32[]{:S(2)}, u32[]{:S(2)}) %collective-permute-start.1) | collective-permute-done | bytes 16416 | tf_op jit(solution)/shard_map/ppermute | solution.py:65
  81.8 0.1 collective-permute-start.2
  81.9 3.1 %collective-permute-done.2 = bf16[1,8,1024]{2,1,0:T(8,128)(2,1)S(1)} collective-permute-done((bf16[1,8,1024]{2,1,0:T(8,128)(2,1)S(1)}, bf16[1,8,1024]{2,1,0:T(8,128)(2,1)S(1)}, u32[]{:S(2)}, u32[]{:S(2)}) %collective-permute-start.2) | collective-permute-done | bytes 16416 | tf_op jit(solution)/shard_map/ppermute | solution.py:65
  85.0 0.0 collective-permute-done.3
  85.0 0.0 collective-permute-done.4
  85.0 0.0 collective-permute-done.5
  85.0 0.0 collective-permute-done.6
  85.1 0.6 gather_fusion
  85.6 0.1 copy.18
  85.7 3.0 %fusion.27 = bf16[2,8,4,1024]{3,1,2,0:T(8,128)(2,1)S(1)} fusion(bf16[2,512,1024]{2,1,0:T(8,128)(2,1)} %param.15, bf16[8,2,4,1024]{3,0,2,1:T(8,128)(2,1)S(1)} %bitcast.133, bf16[2,1024,512]{2,1,0:T(8,128)(2,1)} %param.14), kind=kOutput, calls=%fused_computation.49 | convolution fusion | flops 134578176 | bytes 4456448 | tf_op jit(solution)/shard_map/mesf,efd->mesd/dot_general | solution.py:72
  88.7 0.1 copy.15
  88.8 11.2 %all_to_all.5 = bf16[8,8,1024]{2,1,0:T(8,128)(2,1)S(1)} all-to-all(bf16[8,8,1024]{2,1,0:T(8,128)(2,1)S(1)} %copy.15), channel_id=1, replica_groups=mesh['fc'=8,'tok'=4] {'fc'}, dimensions={0} | all-to-all | bytes 262144 | tf_op jit(solution)/shard_map/all_to_all | solution.py:76
  100.0 9.2 %all_gather.3 = bf16[8,32,1024]{2,1,0:T(8,128)(2,1)S(1)} all-gather(bf16[8,8,1024]{2,1,0:T(8,128)(2,1)S(1)} %all_to_all.5), channel_id=1, replica_groups=mesh['fc'=8,'tok'=4] {'tok'}, dimensions={1}, use_global_device_ids=true | all-gather | bytes 655360 | tf_op jit(solution)/shard_map/all_gather | solution.py:77
  109.2 0.0 copy-start.1
  109.2 2.4 %fusion.2 = bf16[1024,1024]{1,0:T(8,128)(2,1)S(1)} fusion(bf16[1024,1024]{1,0:T(8,128)(2,1)} %bitcast.128, bf16[256,1024]{1,0:T(8,128)(2,1)S(1)} %bitcast.132, f32[1024,256]{0,1:T(8,128)S(1)} %get-tuple-element.70, f32[1024]{0:T(1024)S(1)} %get-tuple-element.5, f32[1024]{0:T(1024)S(1)} %get-tuple-element.69), kind=kOutput, calls=%fused_computation.6 | convolution fusion | flops 540803072 | bytes 5775360 | tf_op jit(solution)/shard_map/dot_general | solution.py:79
  111.6 0.1 fusion.63
  111.7 3.4 %collective-permute-start.8 = (bf16[3,128,1024]{2,1,0:T(8,128)(2,1)S(1)}, bf16[3,128,1024]{2,1,0:T(8,128)(2,1)S(1)}, u32[]{:S(2)}, u32[]{:S(2)}) collective-permute-start(bf16[3,128,1024]{2,1,0:T(8,128)(2,1)S(1)} %bitcast.131), channel_id=1, source_target_pairs={{1,0},{2,1},{3,2},{5,4},{6,5},{7,6},{9,8},{10,9},{11,10},{13,12},{... | collective-permute-start | bytes 2359304 | tf_op jit(solution)/shard_map/ppermute | solution.py:27
  115.1 2.7 %collective-permute-start.7 = (bf16[3,128,1024]{2,1,0:T(8,128)(2,1)S(1)}, bf16[3,128,1024]{2,1,0:T(8,128)(2,1)S(1)}, u32[]{:S(2)}, u32[]{:S(2)}) collective-permute-start(bf16[3,128,1024]{2,1,0:T(8,128)(2,1)S(1)} %bitcast.130), channel_id=1, source_target_pairs={{0,1},{1,2},{2,3},{4,5},{5,6},{6,7},{8,9},{9,10},{10,11},{12,13},{... | collective-permute-start | bytes 2359304 | tf_op jit(solution)/shard_map/ppermute | solution.py:24
  117.8 0.0 copy-done.1
  117.8 0.1 fusion.64
  117.9 0.1 fusion.65
  118.0 15.1 %collective-permute-done.8 = bf16[3,128,1024]{2,1,0:T(8,128)(2,1)S(1)} collective-permute-done((bf16[3,128,1024]{2,1,0:T(8,128)(2,1)S(1)}, bf16[3,128,1024]{2,1,0:T(8,128)(2,1)S(1)}, u32[]{:S(2)}, u32[]{:S(2)}) %collective-permute-start.8) | collective-permute-done | bytes 786464 | tf_op jit(solution)/shard_map/ppermute | solution.py:27
  133.1 15.2 %collective-permute-done.7 = bf16[3,128,1024]{2,1,0:T(8,128)(2,1)S(1)} collective-permute-done((bf16[3,128,1024]{2,1,0:T(8,128)(2,1)S(1)}, bf16[3,128,1024]{2,1,0:T(8,128)(2,1)S(1)}, u32[]{:S(2)}, u32[]{:S(2)}) %collective-permute-start.7) | collective-permute-done | bytes 786464 | tf_op jit(solution)/shard_map/ppermute | solution.py:24
  148.3 2.3 %fusion.14 = (bf16[14,131,1024]{2,1,0:T(8,128)(2,1)S(1)}, bf16[14,131,1024]{2,1,0:T(8,128)(2,1)S(1)}) fusion(bf16[3,128,1024]{2,1,0:T(8,128)(2,1)S(1)} %collective-permute-done.8, bf16[8,128,1024]{2,1,0:T(8,128)(2,1)S(1)} %bitcast.124, bf16[3,128,1024]{2,1,0:T(8,128)(2,1)S(1)} %collective-permute-done.7), kind=kLoop, calls=%fused_computation.25 | loop fusion | flops 45072384 | bytes 11182080 | tf_op jit(solution)/shard_map/concatenate | solution.py:82
  150.6 37.1 %fusion.62 = (f32[8,128]{1,0:T(8,128)S(1)}, f32[8,128,1024]{2,1,0:T(8,128)S(1)}) fusion(f32[1024]{0:T(1024)S(1)} %bitcast.146, bf16[14,131,1024]{2,1,0:T(8,128)(2,1)S(1)} %get-tuple-element.10, f32[1024]{0:T(1024)S(1)} %bitcast.147, f32[1024]{0:T(1024)S(1)} %bitcast.149, f32[1024]{0:T(1024)S(1)} %bitcast.150, ...), kind=kLoop, calls=%fused_computation.101 | loop fusion | flops 160431104 | bytes 96149504 | tf_op jit(solution)/shard_map/reduce_sum | solution.py:91
  187.7 0.0 copy-start.3
  187.7 0.5 multiply_reduce_fusion
  188.3 0.0 copy-start.4
  188.3 0.1 copy-done.3
  188.4 0.6 multiply_convert_fusion
  189.0 0.0 copy-done
  189.0 0.0 copy-done.4
  189.0 4.8 %fusion.12 = bf16[1024,1024]{1,0:T(8,128)(2,1)} fusion(bf16[1024,1024]{1,0:T(8,128)(2,1)S(1)} %fusion.2, f32[1024]{0:T(1024)S(1)} %copy-done.4, bf16[1024,1024]{1,0:T(8,128)(2,1)S(1)} %bitcast.129, bf16[1024,1024]{1,0:T(8,128)(2,1)S(1)} %copy-done), kind=kOutput, calls=%fused_computation.16 | convolution fusion | flops 2160066560 | bytes 8392704 | tf_op jit(solution)/shard_map/dot_general | solution.py:94
  (16 shorter events, 0.1 us)
Async XLA Ops:
  6.5 182.4 %copy-start = (bf16[1024,1024]{1,0:T(8,128)(2,1)S(1)}, bf16[1024,1024]{1,0:T(8,128)(2,1)}, u32[]{:S(2)}) copy-start(bf16[1024,1024]{1,0:T(8,128)(2,1)} %param.18) | copy-start | bytes 6291460
  6.5 63.1 %all-reduce.3.cloned.1.call-start = ((), (), s32[]{:S(2)}) async-start(), calls=%async_computation.1 | async-start | bytes 1048576
  11.4 12.6 %copy-start.5 = (u32[32]{0:T(128)S(1)}, u32[32]{0:T(128)}, u32[]{:S(2)}) copy-start(u32[32]{0:T(128)} %constant.60) | copy-start | bytes 388
  11.4 59.2 %copy-start.2 = (f32[1024]{0:T(1024)S(1)}, f32[1024]{0:T(1024)}, u32[]{:S(2)}) copy-start(f32[1024]{0:T(1024)} %param.13) | copy-start | bytes 12292
  71.7 6.4 %collective-permute-start = (bf16[1,8,1024]{2,1,0:T(8,128)(2,1)S(1)}, bf16[1,8,1024]{2,1,0:T(8,128)(2,1)S(1)}, u32[]{:S(2)}, u32[]{:S(2)}) collective-permute-start(bf16[1,8,1024]{2,1,0:T(8,128)(2,1)S(1)} %get-tuple-element.68), channel_id=1, source_target_pairs={{0,4},{4,0},{8,12},{12,8},{16,20},{20,16},{24,28},{28,24},{1,5},{5... | collective-permute-start | bytes 49160 | tf_op jit(solution)/shard_map/ppermute | solution.py:65
  71.8 13.2 %collective-permute-start.6 = (bf16[1,8,1024]{2,1,0:T(8,128)(2,1)S(1)}, bf16[1,8,1024]{2,1,0:T(8,128)(2,1)S(1)}, u32[]{:S(2)}, u32[]{:S(2)}) collective-permute-start(bf16[1,8,1024]{2,1,0:T(8,128)(2,1)S(1)} %get-tuple-element.62), channel_id=1, source_target_pairs={{0,28},{4,24},{8,20},{12,16},{16,12},{20,8},{24,4},{28,0},{1,29},{... | collective-permute-start | bytes 49160 | tf_op jit(solution)/shard_map/ppermute | solution.py:65
  75.2 9.8 %collective-permute-start.5 = (bf16[1,8,1024]{2,1,0:T(8,128)(2,1)S(1)}, bf16[1,8,1024]{2,1,0:T(8,128)(2,1)S(1)}, u32[]{:S(2)}, u32[]{:S(2)}) collective-permute-start(bf16[1,8,1024]{2,1,0:T(8,128)(2,1)S(1)} %get-tuple-element.63), channel_id=1, source_target_pairs={{0,24},{4,28},{8,16},{12,20},{16,8},{20,12},{24,0},{28,4},{1,25},{... | collective-permute-start | bytes 49160 | tf_op jit(solution)/shard_map/ppermute | solution.py:65
  75.7 9.3 %collective-permute-start.4 = (bf16[1,8,1024]{2,1,0:T(8,128)(2,1)S(1)}, bf16[1,8,1024]{2,1,0:T(8,128)(2,1)S(1)}, u32[]{:S(2)}, u32[]{:S(2)}) collective-permute-start(bf16[1,8,1024]{2,1,0:T(8,128)(2,1)S(1)} %get-tuple-element.64), channel_id=1, source_target_pairs={{0,20},{4,16},{8,28},{12,24},{16,4},{20,0},{24,12},{28,8},{1,21},{... | collective-permute-start | bytes 49160 | tf_op jit(solution)/shard_map/ppermute | solution.py:65
  75.7 9.3 %collective-permute-start.3 = (bf16[1,8,1024]{2,1,0:T(8,128)(2,1)S(1)}, bf16[1,8,1024]{2,1,0:T(8,128)(2,1)S(1)}, u32[]{:S(2)}, u32[]{:S(2)}) collective-permute-start(bf16[1,8,1024]{2,1,0:T(8,128)(2,1)S(1)} %get-tuple-element.65), channel_id=1, source_target_pairs={{0,16},{4,20},{8,24},{12,28},{16,0},{20,4},{24,8},{28,12},{1,17},{... | collective-permute-start | bytes 49160 | tf_op jit(solution)/shard_map/ppermute | solution.py:65
  78.1 3.7 %collective-permute-start.1 = (bf16[1,8,1024]{2,1,0:T(8,128)(2,1)S(1)}, bf16[1,8,1024]{2,1,0:T(8,128)(2,1)S(1)}, u32[]{:S(2)}, u32[]{:S(2)}) collective-permute-start(bf16[1,8,1024]{2,1,0:T(8,128)(2,1)S(1)} %get-tuple-element.67), channel_id=1, source_target_pairs={{0,8},{4,12},{8,0},{12,4},{16,24},{20,28},{24,16},{28,20},{1,9},{5... | collective-permute-start | bytes 49160 | tf_op jit(solution)/shard_map/ppermute | solution.py:65
  81.8 3.2 %collective-permute-start.2 = (bf16[1,8,1024]{2,1,0:T(8,128)(2,1)S(1)}, bf16[1,8,1024]{2,1,0:T(8,128)(2,1)S(1)}, u32[]{:S(2)}, u32[]{:S(2)}) collective-permute-start(bf16[1,8,1024]{2,1,0:T(8,128)(2,1)S(1)} %get-tuple-element.66), channel_id=1, source_target_pairs={{0,12},{4,8},{8,4},{12,0},{16,28},{20,24},{24,20},{28,16},{1,13},{... | collective-permute-start | bytes 49160 | tf_op jit(solution)/shard_map/ppermute | solution.py:65
  109.2 8.6 %copy-start.1 = (f32[7,7,1024]{2,1,0:T(8,128)S(1)}, f32[7,7,1024]{2,1,0:T(8,128)}, u32[]{:S(2)}) copy-start(f32[7,7,1024]{2,1,0:T(8,128)} %param.16) | copy-start | bytes 602116
  111.7 21.4 %collective-permute-start.8 = (bf16[3,128,1024]{2,1,0:T(8,128)(2,1)S(1)}, bf16[3,128,1024]{2,1,0:T(8,128)(2,1)S(1)}, u32[]{:S(2)}, u32[]{:S(2)}) collective-permute-start(bf16[3,128,1024]{2,1,0:T(8,128)(2,1)S(1)} %bitcast.131), channel_id=1, source_target_pairs={{1,0},{2,1},{3,2},{5,4},{6,5},{7,6},{9,8},{10,9},{11,10},{13,12},{... | collective-permute-start | bytes 2359304 | tf_op jit(solution)/shard_map/ppermute | solution.py:27
  115.1 33.2 %collective-permute-start.7 = (bf16[3,128,1024]{2,1,0:T(8,128)(2,1)S(1)}, bf16[3,128,1024]{2,1,0:T(8,128)(2,1)S(1)}, u32[]{:S(2)}, u32[]{:S(2)}) collective-permute-start(bf16[3,128,1024]{2,1,0:T(8,128)(2,1)S(1)} %bitcast.130), channel_id=1, source_target_pairs={{0,1},{1,2},{2,3},{4,5},{5,6},{6,7},{8,9},{9,10},{10,11},{12,13},{... | collective-permute-start | bytes 2359304 | tf_op jit(solution)/shard_map/ppermute | solution.py:24
  187.7 0.7 copy-start.3
  188.3 0.7 copy-start.4
Sparse Core Ops, SparseCore 0:
  24.1 45.4 all-reduce.2
